TPU v7x, 32 devices: a whole 2x2x4 slice. The times are simulated.
32 devices in a mesh: parts: 2 (over y), sht: 4 (over z), det: 2 (over x), sub: 2 (over core).
Axes of the slice: x: 2, y: 2, z: 4, core: 2. Of those that a mesh axis runs over, the one named last changes fastest.
Arguments:
- timestreams: float32 [4, 8, 32, 8192], P(('parts', 'det'), ('sht', 'sub')), parts along dimension 0, may hold values from -96 to 96
- pointing: int32 [4, 8, 8192], P(('parts', 'det'), ('sht', 'sub')), parts along dimension 0, may hold values from 0 to 16383
- noise_weight: float32 [4, 8, 8192], P(('parts', 'det'), ('sht', 'sub')), parts along dimension 0, may hold values from 0.3 to 3
- legendre: float32 [8, 4096, 16], P(('sht', 'sub')), may hold values from -0.09375 to 0.09375
- beam_window: float32 [4096], replicated, may hold values from 0.3 to 1
- prior_weight: float32 [4096], replicated, may hold values from 20 to 2000
Outputs:
- sky_modes: float32 [16, 2, 32, 4096], P(('parts', 'sht', 'sub')), parts along dimension 0
There are 2 independent parts, one for each index of `parts`. A program takes and returns all parts, laid end to end along the dimension named above; an argument that names none is the same for every part. Nothing has to cross between parts.
Inputs may be any that keep to these rules, and one draw needn't show every extreme that they name: `pointing`: each sample falls on a cycle of its own shard: local cycle times 8192 plus azimuth pixel.
All inputs are finite; a program needn't handle non-finite values.
Results may differ from a plain program's by a relative error of at most 0.0001.
Values sent between devices are 32-bit elements; how exact they have to be, the bound alone decides.
A program may use at most 128 MiB of HBM per device.

v0:
```python
import functools
import jax
import jax.numpy as jnp
import numpy as np
from jax import lax
from jax.experimental import pallas as pl
from jax.experimental.pallas import tpu as pltpu
from jax.sharding import PartitionSpec as P

L = 4096
NPHI = 8192
ITERS = 2
LANES = 128


HIGHEST = lax.Precision.HIGHEST


def azimuth_table(numbers):
    columns = jnp.arange(NPHI, dtype=jnp.int32)
    phases = numbers[:, None] * columns[None, :] % NPHI
    angles = phases.astype(jnp.float32) * (2.0 * jnp.pi / NPHI)
    return jnp.stack([2.0 * jnp.cos(angles), -2.0 * jnp.sin(angles)])


def local_inner(left, right):
    return jnp.sum(left * right, axis=(0, 1, 3))


def widen(values):
    return values[None, None, :, None]


def general(timestreams, pointing, noise_weight, legendre, beam_window, prior_weight):
    major_count = lax.axis_size("sht")
    minor_count = lax.axis_size("sub")
    shards = major_count * minor_count
    local_modes = legendre.shape[0]
    modes = local_modes * shards
    cycle_dev = legendre.shape[2] // shards
    pixels = cycle_dev * NPHI
    samples_in = timestreams[0, 0]
    columns = pointing[0, 0]
    weights = noise_weight[0, 0]
    nsims = samples_in.shape[0]
    positions = jnp.arange(modes, dtype=jnp.int32)
    spacing = L // modes
    table = azimuth_table(positions * spacing + spacing // 2)
    stacked_samples = jnp.concatenate([samples_in * weights, weights[None, :]], axis=0)
    binned = jnp.zeros((nsims + 1, pixels), jnp.float32).at[:, columns].add(stacked_samples)
    data_map = binned[:nsims]
    hit_weight = binned[nsims]

    def project(weighted):
        sky = weighted.reshape(nsims, cycle_dev, NPHI)
        cycles = jnp.einsum("srj,cmj->mcsr", sky, table, precision=HIGHEST)
        arrived = lax.all_to_all(cycles, ("sht", "sub"), split_axis=0, concat_axis=3, tiled=True)
        harmonic = jnp.einsum("mcsr,mlr->mcsl", arrived, legendre, precision=HIGHEST)
        harmonic = lax.psum(harmonic, "det")
        return harmonic * beam_window

    def squares(values):
        return lax.psum(local_inner(values, values), ("sht", "sub"))

    rhs = project(data_map)
    solution = jnp.zeros_like(rhs)
    residual = rhs
    direction = rhs
    norm_now = squares(residual)
    for iteration in range(ITERS):
        profile = jnp.einsum("mcsl,mlr->mcsr", direction * beam_window, legendre, precision=HIGHEST)
        synthesize_cycles = lax.all_to_all(
            profile, ("sht", "sub"), split_axis=3, concat_axis=0, tiled=True
        )
        synthesize_sky = jnp.einsum("mcsr,cmj->srj", synthesize_cycles, table, precision=HIGHEST)
        image = (
            project(synthesize_sky.reshape(nsims, pixels) * hit_weight[None, :])
            + prior_weight * direction
        )
        alpha = norm_now / lax.psum(local_inner(direction, image), ("sht", "sub"))
        solution = solution + widen(alpha) * direction
        residual = residual - widen(alpha) * image
        norm_next = squares(residual)
        direction = residual + widen(norm_next / norm_now) * direction
        norm_now = norm_next
    return solution


def phase_matrix(modes, cycles):
    bins = 2 * modes
    angles = np.pi / bins * ((2 * np.arange(modes)[:, None] + 1) * np.arange(bins)[None, :] % (2 * bins))
    table = np.stack([2.0 * np.cos(angles), -2.0 * np.sin(angles)])
    full = np.einsum("ckb,rq->rbckq", table, np.eye(cycles))
    return full.reshape(cycles * bins, 2 * modes * cycles).astype(np.float32)


def dot(left, right):
    return jnp.dot(left, right, precision=HIGHEST, preferred_element_type=jnp.float32)


def dot_t(left, right, **kwargs):
    return lax.dot_general(left, right, (((1,), (1,)), ((), ())),
                           preferred_element_type=jnp.float32, **kwargs)


def turn(values, shift):
    shift = shift % LANES
    return values if shift == 0 else pltpu.roll(values, shift, 1)


def solve_kernel(sizes, stream_hbm, point_hbm, weight_hbm, legendre_hbm, beam_hbm, prior_hbm,
                 phase_hbm, phase_t_hbm, out_ref, basis_ref,
                 stream_ref, point_ref, weight_ref, legendre_ref, beam_ref, prior_ref,
                 phase_ref, phase_t_ref, spread, held, load_sem, send_sem, recv_sem):
    loads = []
    for source, place in ((point_hbm, point_ref), (weight_hbm, weight_ref), (stream_hbm, stream_ref),
                          (legendre_hbm, legendre_ref), (beam_hbm, beam_ref), (prior_hbm, prior_ref),
                          (phase_hbm, phase_ref), (phase_t_hbm, phase_t_ref)):
        load = pltpu.make_async_copy(source, place, load_sem.at[len(loads)])
        load.start()
        loads.append(load)
    modes, cycles, shards, minor, groups, bins, nsims = sizes
    det = lax.axis_index("det")
    shard = lax.axis_index("sht") * minor + lax.axis_index("sub")
    me = det * shards + shard
    count = groups * shards

    def partner(offset):
        other = lax.rem(me + offset, count)
        rest = lax.rem(other, shards)
        return other, {"det": other // shards, "sht": rest // minor, "sub": lax.rem(rest, minor)}

    barrier = pltpu.get_barrier_semaphore()
    for offset in range(1, count):
        pl.semaphore_signal(barrier, inc=1, device_id=partner(offset)[1],
                            device_id_type=pl.DeviceIdType.MESH)

    own = cycles // shards * bins
    for load in loads[:3]:
        load.wait()
    place = point_ref[...]
    column = place & (NPHI - 1)
    sign = (1 - 2 * ((column // bins) & 1)).astype(jnp.float32)
    target = (place // NPHI) * bins + (column & (bins - 1))
    weight = weight_ref[...]
    samples = target.shape[1]
    hot = jnp.where(lax.broadcasted_iota(jnp.int32, (own, samples), 0) == target, 1.0, 0.0)
    hot = hot.astype(jnp.bfloat16)
    rows = jnp.concatenate(
        [stream_ref[...] * (weight * sign), jnp.broadcast_to(weight, (16, samples))], axis=0)
    high = rows.astype(jnp.bfloat16)
    rest = rows - high.astype(jnp.float32)
    middle = rest.astype(jnp.bfloat16)
    low = (rest - middle.astype(jnp.float32)).astype(jnp.bfloat16)
    binned = dot_t(high, hot) + (dot_t(middle, hot) + dot_t(low, hot))

    for load in loads[3:6]:
        load.wait()
    beam = beam_ref[...]
    prior = prior_ref[...]
    power = beam * beam
    center = jnp.sum(power * prior, axis=1, keepdims=True) / jnp.sum(power, axis=1, keepdims=True)
    excess = prior - center
    field = legendre_ref[...] * beam
    upper = det.astype(jnp.float32)
    first = field * ((1.0 - upper) + upper * (excess * excess))
    moments = dot_t(field, jnp.concatenate([first, first * excess], axis=0), precision=HIGHEST)

    spread[...] = jnp.zeros_like(spread)
    spread[0:48, 0:own] = binned
    spread[48:64, 0:own] = moments
    eight = [spread[8 * i:8 * i + 8, :] for i in range(8)]
    held[me, 0:8, :] = (eight[0] + turn(eight[1], 32)) + (turn(eight[2], 64) + turn(eight[3], 96))
    held[me, 8:16, :] = (eight[6] + turn(eight[7], 32)) + turn(eight[4], 64)

    pl.semaphore_wait(barrier, count - 1)
    copies = []
    for offset in range(1, count):
        copy = pltpu.make_async_remote_copy(
            src_ref=held.at[me], dst_ref=held.at[me],
            send_sem=send_sem.at[offset], recv_sem=recv_sem.at[me],
            device_id=partner(offset)[1], device_id_type=pl.DeviceIdType.MESH)
        copy.start()
        copies.append(copy)

    wide = jnp.concatenate([field, field * excess], axis=0)
    wide_high = wide.astype(jnp.bfloat16)
    basis_ref[0:32, :] = wide_high
    basis_ref[32:64, :] = (wide - wide_high.astype(jnp.float32)).astype(jnp.bfloat16)
    basis_ref[64:96, :] = wide_high
    for load in loads[6:]:
        load.wait()
    for offset in range(1, count):
        other, where = partner(offset)
        pltpu.make_async_remote_copy(
            src_ref=held.at[other], dst_ref=held.at[other],
            send_sem=send_sem.at[offset], recv_sem=recv_sem.at[other],
            device_id=where, device_id_type=pl.DeviceIdType.MESH).wait_recv()

    lane = lax.broadcasted_iota(jnp.int32, (8, LANES), 1)
    in_quarter = [lane // 32 == i for i in range(4)]
    in_mode = [lane // cycles == k for k in range(modes)]
    data_half, weight_half = [], []
    for half in range(2):
        data = [held[4 * half + i, 0:8, :] + held[shards + 4 * half + i, 0:8, :] for i in range(4)]
        weights = [held[4 * half + i, 8:16, :] + held[shards + 4 * half + i, 8:16, :] for i in range(4)]

        def gather(parts, at):
            total = jnp.zeros((8, LANES), jnp.float32)
            for i in range(4):
                total = jnp.where(in_quarter[i], turn(parts[i], 32 * (i - at)), total)
            return total

        data_half.append(jnp.concatenate([gather(data, j) for j in range(4)], axis=0))
        weight_half.append(gather(weights, 2))
    data_bins = jnp.concatenate(data_half, axis=1)
    weight_bins = jnp.concatenate(weight_half, axis=1)[0:1, :]
    moment = []
    for n in range(4):
        parts = []
        for k in range(modes):
            got = held[(n // 2) * shards + k, 8:16, :]
            for up in range(2):
                parts.append(jnp.where(in_mode[k], turn(got, cycles * (k - n % 2) - 32 * up), 0.0))
        moment.append(jnp.concatenate(parts, axis=0))

    def stack(values):
        return jnp.concatenate([values[:, :LANES], values[:, LANES:]], axis=0)

    def unstack(values):
        return jnp.concatenate([values[:nsims], values[nsims:]], axis=1)

    def inner(values):
        return jnp.sum(values[:nsims] + values[nsims:], axis=1, keepdims=True)

    def both(values):
        wide = jnp.broadcast_to(values, (nsims, LANES))
        return jnp.concatenate([wide, wide], axis=0)

    def sky(profile):
        return dot(unstack(profile), phase_t_ref[...])

    start = stack(dot(data_bins, phase_ref[...]))
    s0, s1, s2, s3 = [dot(start, m) for m in moment]
    seen = sky(s0)
    weighted = seen * weight_bins
    pulled = stack(dot(weighted, phase_ref[...]))
    g0, g1 = dot(pulled, moment[0]), dot(pulled, moment[1])
    norm = inner(start * s0)
    curve = jnp.sum(seen * weighted, axis=1, keepdims=True) + center * norm + inner(start * s1)
    alpha = norm / curve
    wide_alpha = both(alpha)
    keep = 1.0 - center * wide_alpha
    left = keep * start - wide_alpha * pulled
    left0 = keep * s0 - wide_alpha * g0
    left1 = keep * s1 - wide_alpha * g1
    left_norm = inner(left * (left0 - 2.0 * wide_alpha * s1) + (wide_alpha * wide_alpha) * (start * s2))
    beta = left_norm / norm
    wide_beta = both(beta)
    aim = left + wide_beta * start
    aim0 = left0 + wide_beta * s0
    aim1 = left1 + wide_beta * s1
    seen = sky(aim0 - wide_alpha * s1)
    square = wide_alpha * wide_alpha
    aim_norm = inner(aim * (aim0 - 2.0 * wide_alpha * s1) + square * (start * s2))
    aim_excess = inner(aim * (aim1 - 2.0 * wide_alpha * s2) + square * (start * s3))
    curve = jnp.sum(seen * seen * weight_bins, axis=1, keepdims=True) + center * aim_norm + aim_excess
    step = both(left_norm / curve)
    bent = -(wide_alpha * step) * start
    plain = wide_alpha * start + step * aim

    back = lax.rem(LANES - cycles * shard, LANES)
    wide_lane = lax.broadcasted_iota(jnp.int32, plain.shape, 1)
    factor = jnp.where(
        wide_lane < cycles, pltpu.roll(plain, back, 1),
        jnp.where(wide_lane < 2 * cycles, pltpu.roll(bent, lax.rem(back + cycles, LANES), 1), 0.0))
    factor_high = factor.astype(jnp.bfloat16).astype(jnp.float32)
    out_ref[...] = (factor_high + turn(factor_high, 32)
                    + turn(factor - factor_high, 64)).astype(jnp.bfloat16)
    for copy in copies:
        copy.wait_send()


def expand_kernel(parts, factor_ref, basis_ref, out_hbm, held, sem):
    factor = factor_ref[...][:, :basis_ref.shape[0]]
    width = basis_ref.shape[1] // parts
    copies = []
    for i in range(parts):
        span = pl.ds(i * width, width)
        held[:, span] = jnp.dot(factor, basis_ref[:, span], preferred_element_type=jnp.float32)
        copy = pltpu.make_async_copy(held.at[:, span], out_hbm.at[:, span], sem.at[i])
        copy.start()
        copies.append(copy)
    for copy in copies:
        copy.wait()


def on_device(timestreams, pointing, noise_weight, legendre, beam_window, prior_weight):
    minor = lax.axis_size("sub")
    shards = lax.axis_size("sht") * minor
    groups = lax.axis_size("det")
    modes = legendre.shape[0] * shards
    cycles = legendre.shape[2]
    nsims, samples = timestreams.shape[2:]
    bins = 2 * modes
    if not (modes == shards == 8 and cycles == 16 and groups == 2 and nsims == 32
            and legendre.shape[1] == L and samples % LANES == 0):
        return general(timestreams, pointing, noise_weight, legendre, beam_window, prior_weight)
    count = groups * shards
    flat = jnp.swapaxes(legendre[0], 0, 1)
    beam = beam_window[None, :]
    prior = prior_weight[None, :]
    phase = phase_matrix(modes, cycles)
    sizes = (modes, cycles, shards, minor, groups, bins, nsims)
    vmem = pl.BlockSpec(memory_space=pltpu.VMEM)
    hbm = pl.BlockSpec(memory_space=pltpu.HBM)
    arguments = (timestreams[0, 0], pointing[0], noise_weight[0], flat, beam, prior,
                 jnp.asarray(phase), jnp.asarray(phase.T.copy()))
    factors, basis = pl.pallas_call(
        functools.partial(solve_kernel, sizes),
        out_shape=(jax.ShapeDtypeStruct((2 * nsims, LANES), jnp.bfloat16),
                   jax.ShapeDtypeStruct((6 * cycles, L), jnp.bfloat16)),
        in_specs=[hbm] * 8,
        out_specs=(vmem, vmem),
        scratch_shapes=[pltpu.VMEM(a.shape, a.dtype) for a in arguments] + [
            pltpu.VMEM((64, LANES), jnp.float32),
            pltpu.VMEM((count, 16, LANES), jnp.float32),
            pltpu.SemaphoreType.DMA((len(arguments),)),
            pltpu.SemaphoreType.DMA((count,)),
            pltpu.SemaphoreType.DMA((count,)),
        ],
        compiler_params=pltpu.CompilerParams(
            collective_id=0, has_side_effects=True, vmem_limit_bytes=32 * 2**20),
        name="solve",
    )(*[pltpu.with_memory_space_constraint(a, pltpu.HBM) for a in arguments])
    parts = 4
    expanded = pl.pallas_call(
        functools.partial(expand_kernel, parts),
        out_shape=jax.ShapeDtypeStruct((2 * nsims, L), jnp.float32),
        in_specs=[vmem, vmem],
        out_specs=hbm,
        scratch_shapes=[pltpu.VMEM((2 * nsims, L), jnp.float32), pltpu.SemaphoreType.DMA((parts,))],
        compiler_params=pltpu.CompilerParams(vmem_limit_bytes=16 * 2**20),
        name="expand",
    )(factors, basis)
    return expanded.reshape(1, 2, nsims, L)


def solution(mesh):
    in_specs = (
        P(("parts", "det"), ("sht", "sub"), None, None),
        P(("parts", "det"), ("sht", "sub"), None),
        P(("parts", "det"), ("sht", "sub"), None),
        P(("sht", "sub"), None, None),
        P(),
        P(),
    )
    out_specs = P(("parts", "sht", "sub"), None, None, None)
    return jax.shard_map(
        on_device, mesh=mesh, in_specs=in_specs, out_specs=out_specs, check_vma=False
    )
```

profile of v0, /device:TPU:0, one launch (start us, length us, event | category | flops | bytes accessed | tf_op | source)
XLA Modules:
  0.0 15.1 jit_solution(7370234458657967639)
XLA Ops:
  0.0 13.9 %solve.1 = (bf16[64,128]{1,0:T(8,128)(2,1)S(1)}, bf16[96,4096]{1,0:T(8,128)(2,1)S(1)}) custom-call(f32[32,8192]{1,0:T(8,128)} %bitcast.9, s32[1,8192]{1,0:T(1,128)} %bitcast.11, f32[1,8192]{1,0:T(1,128)} %bitcast.12, f32[16,4096]{1,0:T(8,128)} %bitcast.10, f32[1,4096]{1,0:T(1,128)} %bitcast.13, f32[1,4096]{1,0:T(1,128)} %bitcast.14, ...), custom_call_target="tpu_custom_call" | custom-call | tf_op jit(solution)/shard_map/solve/pallas_call | solution.py:319
  13.9 1.2 %expand.1 = f32[64,4096]{1,0:T(8,128)} custom-call(bf16[64,128]{1,0:T(8,128)(2,1)S(1)} %get-tuple-element.7.factor_ref, bf16[96,4096]{1,0:T(8,128)(2,1)S(1)} %get-tuple-element.8.basis_ref), custom_call_target="tpu_custom_call" | custom-call | tf_op jit(solution)/shard_map/expand/pallas_call | solution.py:337
where the time goes:
time: 15.2 us; the launch traced here: 15.1 us
  Pallas kernels  15 us (99%)
    pallas_call x1, Pallas kernels, on_device(): pl.pallas_call(functools.partial(solve_kernel, sizes), out_shape=(jax.Sha...  13.9 us
    pallas_call x1, Pallas kernels, on_device(): pl.pallas_call(functools.partial(expand_kernel, parts), out_shape=jax.Sha...  1.17 us

commit v1 on v0

--- a/solution.py
+++ b/solution.py
@@ -1,6 +1,7 @@
 import functools
 import jax
 import jax.numpy as jnp
+import ml_dtypes
 import numpy as np
 from jax import lax
 from jax.experimental import pallas as pl
@@ -94,67 +95,74 @@
     return full.reshape(cycles * bins, 2 * modes * cycles).astype(np.float32)
 
 
-def dot(left, right):
-    return jnp.dot(left, right, precision=HIGHEST, preferred_element_type=jnp.float32)
-
-
 def dot_t(left, right, **kwargs):
     return lax.dot_general(left, right, (((1,), (1,)), ((), ())),
                            preferred_element_type=jnp.float32, **kwargs)
 
 
+def split(values, count):
+    parts = []
+    for _ in range(count):
+        parts.append(values.astype(jnp.bfloat16))
+        values = values - parts[-1].astype(jnp.float32)
+    return parts
+
+
+def split_dot(left, right):
+    count = len(right)
+    rows = left.shape[0]
+    parts = split(left, count)
+    total = None
+    for i in reversed(range(count)):
+        got = jnp.dot(jnp.concatenate(parts[:count - i], axis=0), right[i],
+                      preferred_element_type=jnp.float32)
+        for j in reversed(range(count - i)):
+            piece = got[j * rows:(j + 1) * rows]
+            total = piece if total is None else total + piece
+    return total
+
+
 def turn(values, shift):
     shift = shift % LANES
     return values if shift == 0 else pltpu.roll(values, shift, 1)
 
 
 def solve_kernel(sizes, stream_hbm, point_hbm, weight_hbm, legendre_hbm, beam_hbm, prior_hbm,
-                 phase_hbm, phase_t_hbm, out_ref, basis_ref,
+                 phase_hbm, out_ref, basis_ref,
                  stream_ref, point_ref, weight_ref, legendre_ref, beam_ref, prior_ref,
-                 phase_ref, phase_t_ref, spread, held, load_sem, send_sem, recv_sem):
-    loads = []
-    for source, place in ((point_hbm, point_ref), (weight_hbm, weight_ref), (stream_hbm, stream_ref),
-                          (legendre_hbm, legendre_ref), (beam_hbm, beam_ref), (prior_hbm, prior_ref),
-                          (phase_hbm, phase_ref), (phase_t_hbm, phase_t_ref)):
-        load = pltpu.make_async_copy(source, place, load_sem.at[len(loads)])
+                 phase_ref, spread, held, load_sem, send_sem, recv_sem):
+    modes, cycles, shards, minor, groups, bins, nsims, cuts = sizes
+    samples = point_ref.shape[1]
+    span = samples // cuts
+    chunks = [pl.ds(i * span, span) for i in range(cuts)]
+    pairs = [(legendre_hbm, legendre_ref), (beam_hbm, beam_ref), (prior_hbm, prior_ref),
+             (point_hbm, point_ref), (weight_hbm, weight_ref)]
+    pairs += [(stream_hbm.at[:, c], stream_ref.at[:, c]) for c in chunks]
+    pairs += [(phase_hbm, phase_ref)]
+    loads = [pltpu.make_async_copy(source, place, load_sem.at[i])
+             for i, (source, place) in enumerate(pairs)]
+    for load in loads:
         load.start()
-        loads.append(load)
-    modes, cycles, shards, minor, groups, bins, nsims = sizes
     det = lax.axis_index("det")
-    shard = lax.axis_index("sht") * minor + lax.axis_index("sub")
+    major, sub = lax.axis_index("sht"), lax.axis_index("sub")
+    majors = shards // minor
+    shard = major * minor + sub
     me = det * shards + shard
     count = groups * shards
 
     def partner(offset):
-        other = lax.rem(me + offset, count)
-        rest = lax.rem(other, shards)
-        return other, {"det": other // shards, "sht": rest // minor, "sub": lax.rem(rest, minor)}
+        step = offset // (groups * minor)
+        row = step + (step - major + majors) // majors if step < majors - 1 else major
+        side = lax.rem(det + 1 + offset // minor, groups)
+        core = lax.rem(sub + 1 + offset, minor)
+        return side * shards + row * minor + core, {"det": side, "sht": row, "sub": core}
 
     barrier = pltpu.get_barrier_semaphore()
-    for offset in range(1, count):
+    for offset in range(count - 1):
         pl.semaphore_signal(barrier, inc=1, device_id=partner(offset)[1],
                             device_id_type=pl.DeviceIdType.MESH)
 
-    own = cycles // shards * bins
     for load in loads[:3]:
-        load.wait()
-    place = point_ref[...]
-    column = place & (NPHI - 1)
-    sign = (1 - 2 * ((column // bins) & 1)).astype(jnp.float32)
-    target = (place // NPHI) * bins + (column & (bins - 1))
-    weight = weight_ref[...]
-    samples = target.shape[1]
-    hot = jnp.where(lax.broadcasted_iota(jnp.int32, (own, samples), 0) == target, 1.0, 0.0)
-    hot = hot.astype(jnp.bfloat16)
-    rows = jnp.concatenate(
-        [stream_ref[...] * (weight * sign), jnp.broadcast_to(weight, (16, samples))], axis=0)
-    high = rows.astype(jnp.bfloat16)
-    rest = rows - high.astype(jnp.float32)
-    middle = rest.astype(jnp.bfloat16)
-    low = (rest - middle.astype(jnp.float32)).astype(jnp.bfloat16)
-    binned = dot_t(high, hot) + (dot_t(middle, hot) + dot_t(low, hot))
-
-    for load in loads[3:6]:
         load.wait()
     beam = beam_ref[...]
     prior = prior_ref[...]
@@ -164,18 +172,41 @@
     field = legendre_ref[...] * beam
     upper = det.astype(jnp.float32)
     first = field * ((1.0 - upper) + upper * (excess * excess))
-    moments = dot_t(field, jnp.concatenate([first, first * excess], axis=0), precision=HIGHEST)
-
-    spread[...] = jnp.zeros_like(spread)
+    left = jnp.concatenate(split(field, 3), axis=0)
+    right = jnp.concatenate(split(jnp.concatenate([first, first * excess], axis=0), 3), axis=0)
+    crossed = dot_t(left, right)
+    top, mid, end = crossed[0:16], crossed[16:32], crossed[32:48]
+    spread[64:112, 0:96] = jnp.concatenate([top + (mid + end), top + mid, top], axis=0)
+
+    for load in loads[3:5]:
+        load.wait()
+    own = cycles // shards * bins
+    binned = jnp.zeros((96, own), jnp.float32)
+    for chunk, load in zip(chunks, loads[5:5 + cuts]):
+        place = point_ref[:, chunk]
+        column = place & (NPHI - 1)
+        sign = (1 - 2 * ((column // bins) & 1)).astype(jnp.float32)
+        target = (place // NPHI) * bins + (column & (bins - 1))
+        weight = weight_ref[:, chunk]
+        hot = jnp.where(lax.broadcasted_iota(jnp.int32, (own, span), 0) == target, 1.0, 0.0)
+        hot = hot.astype(jnp.bfloat16)
+        load.wait()
+        rows = jnp.concatenate(
+            [stream_ref[:, chunk] * (weight * sign), jnp.broadcast_to(weight, (16, span))], axis=0)
+        binned += dot_t(jnp.concatenate(split(rows, 2), axis=0), hot)
+    binned = binned[0:48] + binned[48:96]
+
+    spread[0:64] = jnp.zeros((64, LANES), jnp.float32)
     spread[0:48, 0:own] = binned
-    spread[48:64, 0:own] = moments
+    spread[48:64, 0:32] = spread[64:80, 0:32] + (
+        turn(spread[80:96, :], -32) + turn(spread[96:112, :], -64))[:, 0:32]
     eight = [spread[8 * i:8 * i + 8, :] for i in range(8)]
     held[me, 0:8, :] = (eight[0] + turn(eight[1], 32)) + (turn(eight[2], 64) + turn(eight[3], 96))
     held[me, 8:16, :] = (eight[6] + turn(eight[7], 32)) + turn(eight[4], 64)
 
     pl.semaphore_wait(barrier, count - 1)
     copies = []
-    for offset in range(1, count):
+    for offset in range(count - 1):
         copy = pltpu.make_async_remote_copy(
             src_ref=held.at[me], dst_ref=held.at[me],
             send_sem=send_sem.at[offset], recv_sem=recv_sem.at[me],
@@ -188,9 +219,8 @@
     basis_ref[0:32, :] = wide_high
     basis_ref[32:64, :] = (wide - wide_high.astype(jnp.float32)).astype(jnp.bfloat16)
     basis_ref[64:96, :] = wide_high
-    for load in loads[6:]:
-        load.wait()
-    for offset in range(1, count):
+    loads[-1].wait()
+    for offset in range(count - 1):
         other, where = partner(offset)
         pltpu.make_async_remote_copy(
             src_ref=held.at[other], dst_ref=held.at[other],
@@ -237,34 +267,45 @@
         wide = jnp.broadcast_to(values, (nsims, LANES))
         return jnp.concatenate([wide, wide], axis=0)
 
+    size = 2 * modes * cycles
+    phase = [phase_ref[i * size:(i + 1) * size, :] for i in range(4)]
+
     def sky(profile):
-        return dot(unstack(profile), phase_t_ref[...])
-
-    start = stack(dot(data_bins, phase_ref[...]))
-    s0, s1, s2, s3 = [dot(start, m) for m in moment]
+        return split_dot(unstack(profile), phase[2:])
+
+    def profiles(bins_in):
+        return stack(split_dot(bins_in, phase[:2]))
+
+    moment_parts = split(jnp.concatenate(moment, axis=1), 3)
+    start = profiles(data_bins)
+    applied = split_dot(start, moment_parts)
+    s0, s1, s2, s3 = [applied[:, n * LANES:(n + 1) * LANES] for n in range(4)]
     seen = sky(s0)
     weighted = seen * weight_bins
-    pulled = stack(dot(weighted, phase_ref[...]))
-    g0, g1 = dot(pulled, moment[0]), dot(pulled, moment[1])
+    pulled = profiles(weighted)
+    applied = split_dot(pulled, [part[:, :2 * LANES] for part in moment_parts])
+    g0, g1 = applied[:, :LANES], applied[:, LANES:]
+    seen_more = sky(g0 + s1)
     norm = inner(start * s0)
     curve = jnp.sum(seen * weighted, axis=1, keepdims=True) + center * norm + inner(start * s1)
     alpha = norm / curve
     wide_alpha = both(alpha)
+    square = wide_alpha * wide_alpha
     keep = 1.0 - center * wide_alpha
     left = keep * start - wide_alpha * pulled
     left0 = keep * s0 - wide_alpha * g0
     left1 = keep * s1 - wide_alpha * g1
-    left_norm = inner(left * (left0 - 2.0 * wide_alpha * s1) + (wide_alpha * wide_alpha) * (start * s2))
+    left_norm = inner(left * (left0 - 2.0 * wide_alpha * s1) + square * (start * s2))
     beta = left_norm / norm
     wide_beta = both(beta)
     aim = left + wide_beta * start
     aim0 = left0 + wide_beta * s0
     aim1 = left1 + wide_beta * s1
-    seen = sky(aim0 - wide_alpha * s1)
-    square = wide_alpha * wide_alpha
+    aim_seen = (1.0 - center * alpha + beta) * seen - alpha * seen_more
     aim_norm = inner(aim * (aim0 - 2.0 * wide_alpha * s1) + square * (start * s2))
     aim_excess = inner(aim * (aim1 - 2.0 * wide_alpha * s2) + square * (start * s3))
-    curve = jnp.sum(seen * seen * weight_bins, axis=1, keepdims=True) + center * aim_norm + aim_excess
+    curve = (jnp.sum(aim_seen * aim_seen * weight_bins, axis=1, keepdims=True)
+             + center * aim_norm + aim_excess)
     step = both(left_norm / curve)
     bent = -(wide_alpha * step) * start
     plain = wide_alpha * start + step * aim
@@ -304,28 +345,32 @@
     nsims, samples = timestreams.shape[2:]
     bins = 2 * modes
     if not (modes == shards == 8 and cycles == 16 and groups == 2 and nsims == 32
-            and legendre.shape[1] == L and samples % LANES == 0):
+            and legendre.shape[1] == L and samples % (4 * LANES) == 0):
         return general(timestreams, pointing, noise_weight, legendre, beam_window, prior_weight)
     count = groups * shards
     flat = jnp.swapaxes(legendre[0], 0, 1)
     beam = beam_window[None, :]
     prior = prior_weight[None, :]
-    phase = phase_matrix(modes, cycles)
-    sizes = (modes, cycles, shards, minor, groups, bins, nsims)
+    full = phase_matrix(modes, cycles)
+    high = full.astype(ml_dtypes.bfloat16)
+    low = (full - high.astype(np.float32)).astype(ml_dtypes.bfloat16)
+    phase = np.concatenate([high, low, high.T, low.T], axis=0)
+    cuts = 1
+    sizes = (modes, cycles, shards, minor, groups, bins, nsims, cuts)
     vmem = pl.BlockSpec(memory_space=pltpu.VMEM)
     hbm = pl.BlockSpec(memory_space=pltpu.HBM)
     arguments = (timestreams[0, 0], pointing[0], noise_weight[0], flat, beam, prior,
-                 jnp.asarray(phase), jnp.asarray(phase.T.copy()))
+                 jnp.asarray(phase))
     factors, basis = pl.pallas_call(
         functools.partial(solve_kernel, sizes),
         out_shape=(jax.ShapeDtypeStruct((2 * nsims, LANES), jnp.bfloat16),
                    jax.ShapeDtypeStruct((6 * cycles, L), jnp.bfloat16)),
-        in_specs=[hbm] * 8,
+        in_specs=[hbm] * 7,
         out_specs=(vmem, vmem),
         scratch_shapes=[pltpu.VMEM(a.shape, a.dtype) for a in arguments] + [
-            pltpu.VMEM((64, LANES), jnp.float32),
+            pltpu.VMEM((112, LANES), jnp.float32),
             pltpu.VMEM((count, 16, LANES), jnp.float32),
-            pltpu.SemaphoreType.DMA((len(arguments),)),
+            pltpu.SemaphoreType.DMA((len(arguments) + cuts - 1,)),
             pltpu.SemaphoreType.DMA((count,)),
             pltpu.SemaphoreType.DMA((count,)),
         ],

time: 15.2 us -> 13.7 us (0.901)
  Pallas kernels: 15 us -> 13.6 us
    pallas_call x1, Pallas kernels: 13.9 us -> 12.4 us  [on_device(): pl.pallas_call(functools.partial(solve_kernel, sizes), out_shape=(jax.Sha...]
where the time goes in v1:
time: 13.7 us; the launch traced here: 13.6 us
  Pallas kernels  13.6 us (99%)
    pallas_call x1, Pallas kernels, on_device(): pl.pallas_call(functools.partial(solve_kernel, sizes), out_shape=(jax.Sha...  12.4 us
    pallas_call x1, Pallas kernels, on_device(): pl.pallas_call(functools.partial(expand_kernel, parts), out_shape=jax.Sha...  1.18 us

profile of v1, /device:TPU:0, one launch (start us, length us, event | category | flops | bytes accessed | tf_op | source)
XLA Modules:
  0.0 13.6 jit_solution(4255294257525184259)
XLA Ops:
  0.0 12.4 %solve.1 = (bf16[64,128]{1,0:T(8,128)(2,1)S(1)}, bf16[96,4096]{1,0:T(8,128)(2,1)S(1)}) custom-call(f32[32,8192]{1,0:T(8,128)} %bitcast.9, s32[1,8192]{1,0:T(1,128)} %bitcast.11, f32[1,8192]{1,0:T(1,128)} %bitcast.12, f32[16,4096]{1,0:T(8,128)} %bitcast.10, f32[1,4096]{1,0:T(1,128)} %bitcast.13, f32[1,4096]{1,0:T(1,128)} %bitcast.14, ...), custom_call_target="tpu_custom_call" | custom-call | tf_op jit(solution)/shard_map/solve/pallas_call | solution.py:364
  12.4 1.2 %expand.1 = f32[64,4096]{1,0:T(8,128)} custom-call(bf16[64,128]{1,0:T(8,128)(2,1)S(1)} %get-tuple-element.7.factor_ref, bf16[96,4096]{1,0:T(8,128)(2,1)S(1)} %get-tuple-element.8.basis_ref), custom_call_target="tpu_custom_call" | custom-call | tf_op jit(solution)/shard_map/expand/pallas_call | solution.py:382

commit v2 on v1

--- a/solution.py
+++ b/solution.py
@@ -133,11 +133,11 @@
                  phase_ref, spread, held, load_sem, send_sem, recv_sem):
     modes, cycles, shards, minor, groups, bins, nsims, cuts = sizes
     samples = point_ref.shape[1]
-    span = samples // cuts
-    chunks = [pl.ds(i * span, span) for i in range(cuts)]
     pairs = [(legendre_hbm, legendre_ref), (beam_hbm, beam_ref), (prior_hbm, prior_ref),
              (point_hbm, point_ref), (weight_hbm, weight_ref)]
-    pairs += [(stream_hbm.at[:, c], stream_ref.at[:, c]) for c in chunks]
+    height = nsims // cuts
+    pairs += [(stream_hbm.at[pl.ds(i * height, height)], stream_ref.at[pl.ds(i * height, height)])
+              for i in range(cuts)]
     pairs += [(phase_hbm, phase_ref)]
     loads = [pltpu.make_async_copy(source, place, load_sem.at[i])
              for i, (source, place) in enumerate(pairs)]
@@ -162,7 +162,7 @@
         pl.semaphore_signal(barrier, inc=1, device_id=partner(offset)[1],
                             device_id_type=pl.DeviceIdType.MESH)
 
-    for load in loads[:3]:
+    for load in loads[:-1]:
         load.wait()
     beam = beam_ref[...]
     prior = prior_ref[...]
@@ -178,22 +178,17 @@
     top, mid, end = crossed[0:16], crossed[16:32], crossed[32:48]
     spread[64:112, 0:96] = jnp.concatenate([top + (mid + end), top + mid, top], axis=0)
 
-    for load in loads[3:5]:
-        load.wait()
     own = cycles // shards * bins
-    binned = jnp.zeros((96, own), jnp.float32)
-    for chunk, load in zip(chunks, loads[5:5 + cuts]):
-        place = point_ref[:, chunk]
-        column = place & (NPHI - 1)
-        sign = (1 - 2 * ((column // bins) & 1)).astype(jnp.float32)
-        target = (place // NPHI) * bins + (column & (bins - 1))
-        weight = weight_ref[:, chunk]
-        hot = jnp.where(lax.broadcasted_iota(jnp.int32, (own, span), 0) == target, 1.0, 0.0)
-        hot = hot.astype(jnp.bfloat16)
-        load.wait()
-        rows = jnp.concatenate(
-            [stream_ref[:, chunk] * (weight * sign), jnp.broadcast_to(weight, (16, span))], axis=0)
-        binned += dot_t(jnp.concatenate(split(rows, 2), axis=0), hot)
+    place = point_ref[...]
+    column = place & (NPHI - 1)
+    sign = (1 - 2 * ((column // bins) & 1)).astype(jnp.float32)
+    target = (place // NPHI) * bins + (column & (bins - 1))
+    weight = weight_ref[...]
+    hot = jnp.where(lax.broadcasted_iota(jnp.int32, (own, samples), 0) == target, 1.0, 0.0)
+    hot = hot.astype(jnp.bfloat16)
+    rows = jnp.concatenate(
+        [stream_ref[...] * (weight * sign), jnp.broadcast_to(weight, (16, samples))], axis=0)
+    binned = dot_t(jnp.concatenate(split(rows, 2), axis=0), hot)
     binned = binned[0:48] + binned[48:96]
 
     spread[0:64] = jnp.zeros((64, LANES), jnp.float32)
@@ -345,7 +340,7 @@
     nsims, samples = timestreams.shape[2:]
     bins = 2 * modes
     if not (modes == shards == 8 and cycles == 16 and groups == 2 and nsims == 32
-            and legendre.shape[1] == L and samples % (4 * LANES) == 0):
+            and legendre.shape[1] == L and samples % LANES == 0):
         return general(timestreams, pointing, noise_weight, legendre, beam_window, prior_weight)
     count = groups * shards
     flat = jnp.swapaxes(legendre[0], 0, 1)

time: 13.7 us -> 13.3 us (0.971)
  Pallas kernels: 13.6 us -> 13.2 us
    pallas_call x1, Pallas kernels: 12.4 us -> 12 us  [on_device(): pl.pallas_call(functools.partial(solve_kernel, sizes), out_shape=(jax.Sha...]
where the time goes in v2:
time: 13.3 us; the launch traced here: 13.2 us
  Pallas kernels  13.2 us (99%)
    pallas_call x1, Pallas kernels, on_device(): pl.pallas_call(functools.partial(solve_kernel, sizes), out_shape=(jax.Sha...  12 us
    pallas_call x1, Pallas kernels, on_device(): pl.pallas_call(functools.partial(expand_kernel, parts), out_shape=jax.Sha...  1.18 us

profile of v2, /device:TPU:0, one launch (start us, length us, event | category | flops | bytes accessed | tf_op | source)
XLA Modules:
  0.0 13.2 jit_solution(9662777856810687488)
XLA Ops:
  0.0 12.0 %solve.1 = (bf16[64,128]{1,0:T(8,128)(2,1)S(1)}, bf16[96,4096]{1,0:T(8,128)(2,1)S(1)}) custom-call(f32[32,8192]{1,0:T(8,128)} %bitcast.9, s32[1,8192]{1,0:T(1,128)} %bitcast.11, f32[1,8192]{1,0:T(1,128)} %bitcast.12, f32[16,4096]{1,0:T(8,128)} %bitcast.10, f32[1,4096]{1,0:T(1,128)} %bitcast.13, f32[1,4096]{1,0:T(1,128)} %bitcast.14, ...), custom_call_target="tpu_custom_call" | custom-call | tf_op jit(solution)/shard_map/solve/pallas_call | solution.py:359
  12.0 1.2 %expand.1 = f32[64,4096]{1,0:T(8,128)} custom-call(bf16[64,128]{1,0:T(8,128)(2,1)S(1)} %get-tuple-element.7.factor_ref, bf16[96,4096]{1,0:T(8,128)(2,1)S(1)} %get-tuple-element.8.basis_ref), custom_call_target="tpu_custom_call" | custom-call | tf_op jit(solution)/shard_map/expand/pallas_call | solution.py:377

commit v3 on v2

--- a/solution.py
+++ b/solution.py
@@ -186,10 +186,13 @@
     weight = weight_ref[...]
     hot = jnp.where(lax.broadcasted_iota(jnp.int32, (own, samples), 0) == target, 1.0, 0.0)
     hot = hot.astype(jnp.bfloat16)
-    rows = jnp.concatenate(
-        [stream_ref[...] * (weight * sign), jnp.broadcast_to(weight, (16, samples))], axis=0)
-    binned = dot_t(jnp.concatenate(split(rows, 2), axis=0), hot)
-    binned = binned[0:48] + binned[48:96]
+    upper_half = lax.broadcasted_iota(jnp.int32, (16, samples), 0) < 8
+    weight_high = weight.astype(jnp.bfloat16).astype(jnp.float32)
+    weight_rows = jnp.where(upper_half, weight_high, weight - weight_high).astype(jnp.bfloat16)
+    rows = split(stream_ref[...] * (weight * sign), 2) + [weight_rows]
+    binned = dot_t(jnp.concatenate(rows, axis=0), hot)
+    weight_sum = binned[64:72] + binned[72:80]
+    binned = jnp.concatenate([binned[0:32] + binned[32:64], weight_sum, weight_sum], axis=0)
 
     spread[0:64] = jnp.zeros((64, LANES), jnp.float32)
     spread[0:48, 0:own] = binned

time: 13.3 us -> 13.2 us (level)
  no operation moved by 1% of the time
where the time goes in v3:
time: 13.2 us; the launch traced here: 13.1 us
  Pallas kernels  13.1 us (99%)
    pallas_call x1, Pallas kernels, on_device(): pl.pallas_call(functools.partial(solve_kernel, sizes), out_shape=(jax.Sha...  11.9 us
    pallas_call x1, Pallas kernels, on_device(): pl.pallas_call(functools.partial(expand_kernel, parts), out_shape=jax.Sha...  1.18 us

profile of v3, /device:TPU:0, one launch (start us, length us, event | category | flops | bytes accessed | tf_op | source)
XLA Modules:
  0.0 13.1 jit_solution(12748850109039210424)
XLA Ops:
  0.0 11.9 %solve.1 = (bf16[64,128]{1,0:T(8,128)(2,1)S(1)}, bf16[96,4096]{1,0:T(8,128)(2,1)S(1)}) custom-call(f32[32,8192]{1,0:T(8,128)} %bitcast.9, s32[1,8192]{1,0:T(1,128)} %bitcast.11, f32[1,8192]{1,0:T(1,128)} %bitcast.12, f32[16,4096]{1,0:T(8,128)} %bitcast.10, f32[1,4096]{1,0:T(1,128)} %bitcast.13, f32[1,4096]{1,0:T(1,128)} %bitcast.14, ...), custom_call_target="tpu_custom_call" | custom-call | tf_op jit(solution)/shard_map/solve/pallas_call | solution.py:362
  11.9 1.2 %expand.1 = f32[64,4096]{1,0:T(8,128)} custom-call(bf16[64,128]{1,0:T(8,128)(2,1)S(1)} %get-tuple-element.7.factor_ref, bf16[96,4096]{1,0:T(8,128)(2,1)S(1)} %get-tuple-element.8.basis_ref), custom_call_target="tpu_custom_call" | custom-call | tf_op jit(solution)/shard_map/expand/pallas_call | solution.py:380
